TPU v7x, 32 devices: a whole 2x2x4 slice. The times are simulated.
32 devices in a mesh: section: 4 (over y, x), dp: 8 (over z, core).
Axes of the slice: x: 2, y: 2, z: 4, core: 2. Of those that a mesh axis runs over, the one named last changes fastest.
Arguments:
- images: bfloat16 [16, 16, 16, 768], P('dp'), may hold values from -6 to 6
- roster: int32 [8, 2], P('dp'), may hold values from 0 to 1, each once within a row
- cotangent: bfloat16 [16, 16, 16, 768], P('dp'), may hold values from -6 to 6
- depth_kernel: bfloat16 [4, 7, 7, 768], P('section'), may hold values from -0.875 to 0.875
- up_weight: bfloat16 [4, 768, 3072], P('section'), may hold values from -0.21875 to 0.21875
- down_weight: bfloat16 [4, 3072, 768], P('section'), may hold values from -0.109375 to 0.109375
- layer_scale: float32 [4, 768], P('section'), may hold values from 0.3 to 1
- master: float32 [4, 55752, 128], P('section', 'dp'), may hold values from -0.75 to 0.75
- first_moment: float32 [4, 55752, 128], P('section', 'dp'), may hold values from -6 to 6
- second_moment: float32 [4, 55752, 128], P('section', 'dp'), may hold values from 0.05 to 5
- bucket_bounds: int32 [4, 25], P('section'), may hold values from 0 to 37168, as said below
- bucket_owner: int32 [4, 24], P('section'), may hold values from 0 to 7, as said below
Outputs:
- section_outputs: bfloat16 [4, 16, 16, 16, 768], P('section', 'dp')
- new_master: float32 [4, 55752, 128], P('section', 'dp')
- new_first_moment: float32 [4, 55752, 128], P('section', 'dp')
- new_second_moment: float32 [4, 55752, 128], P('section', 'dp')
Inputs may be any that keep to these rules, and one draw needn't show every extreme that they name: `roster`: each row names every slot once. `bucket_bounds`: in each block's row the bounds never fall, the first is 0 and the last is 37168. `bucket_owner`: in each block every owner is named by 3 buckets; the buckets of one owner hold at most 6969 rows together, and some owner holds exactly 6969.
All inputs are finite; a program needn't handle non-finite values.
Results may differ from a plain program's by a relative error of at most 0.028.
Values may be sent and summed in bfloat16 or wider, within the bound.
A program may use at most 128 MiB of HBM per device.

v0:
```python
import jax
import jax.numpy as jnp
from jax import lax
from jax.sharding import PartitionSpec as P

GRAN = 128


beta_one = 0.9
beta_two = 0.95
learn_rate = 0.01
decay_rate = 0.1
adam_eps = 1e-08
norm_eps = 1e-06
first_fix = 1.0 - 0.9**10
second_fix = 1.0 - 0.95**10


def shifted(block, axis, distance):
    devices = range(lax.axis_size(axis))
    route = [(i - distance, i) for i in devices if i - distance in devices]
    return lax.ppermute(block, axis, route)


def depthwise(inputs, kernel):
    reach = (kernel.shape[0] - 1) // 2
    return lax.conv_general_dilated(
        inputs,
        kernel[:, :, None, :],
        (1, 1),
        ((reach, reach), (reach, reach)),
        dimension_numbers=("NHWC", "HWIO", "NHWC"),
        feature_group_count=inputs.shape[-1],
        preferred_element_type=jnp.float32,
    )


def gelu_slope(values):
    cumulative = 0.5 * (1.0 + lax.erf(values * 0.7071067811865476))
    return cumulative + values * jnp.exp(-0.5 * values * values) * 0.3989422804014327


def normalize(conv_rows):
    centred = conv_rows - jnp.mean(conv_rows, axis=-1, keepdims=True)
    inv_std = lax.rsqrt(jnp.mean(centred * centred, axis=-1, keepdims=True) + norm_eps)
    return (centred * inv_std, inv_std)


def block_forward(block_in, kernel, up_matrix, down_matrix, scale_row):
    channels = block_in.shape[-1]
    conv_rows = depthwise(block_in, kernel).reshape(-1, channels)
    normed_f, inv_std = normalize(conv_rows)
    normed = normed_f.astype(jnp.bfloat16)
    hidden_pre = jnp.dot(normed, up_matrix, preferred_element_type=jnp.float32)
    hidden = jax.nn.gelu(hidden_pre, approximate=False).astype(jnp.bfloat16)
    branch = jnp.dot(hidden, down_matrix, preferred_element_type=jnp.float32)
    block_out = block_in.reshape(-1, channels).astype(jnp.float32) + scale_row * branch
    return (block_out.astype(jnp.bfloat16).reshape(block_in.shape), conv_rows, hidden_pre, branch)


def block_backward(
    grad_out, block_in, conv_rows, hidden_pre, branch, kernel, up_matrix, down_matrix, scale_row
):
    channels = block_in.shape[-1]
    out_rows = grad_out.reshape(-1, channels).astype(jnp.float32)
    scaled = (out_rows * scale_row).astype(jnp.bfloat16)
    scale_terms = out_rows * branch
    hidden = jax.nn.gelu(hidden_pre, approximate=False).astype(jnp.bfloat16)
    grad_hidden = lax.dot_general(
        scaled, down_matrix, (((1,), (1,)), ((), ())), preferred_element_type=jnp.float32
    )
    grad_pre = (grad_hidden * gelu_slope(hidden_pre)).astype(jnp.bfloat16)
    normed_f, inv_std = normalize(conv_rows)
    normed = normed_f.astype(jnp.bfloat16)
    grad_normed = lax.dot_general(
        grad_pre, up_matrix, (((1,), (1,)), ((), ())), preferred_element_type=jnp.float32
    )
    grad_conv = inv_std * (
        grad_normed
        - jnp.mean(grad_normed, axis=-1, keepdims=True)
        - normed_f * jnp.mean(grad_normed * normed_f, axis=-1, keepdims=True)
    )
    grad_conv = grad_conv.astype(jnp.bfloat16).reshape(block_in.shape)
    back_conv = depthwise(grad_conv, kernel[::-1, ::-1])
    grad_in = (
        (out_rows + back_conv.reshape(-1, channels)).astype(jnp.bfloat16).reshape(block_in.shape)
    )
    return (grad_in, scaled, hidden, grad_pre, normed, grad_conv, scale_terms)


def kernel_grad(block_in, grad_conv, kernel):
    reach = (kernel.shape[0] - 1) // 2
    padded = jnp.pad(block_in, ((reach, reach), (reach, reach), (0, 0)))
    return lax.conv_general_dilated(
        padded[None],
        grad_conv[:, :, None, :],
        (1, 1),
        ((0, 0), (0, 0)),
        dimension_numbers=("NHWC", "HWIO", "NHWC"),
        feature_group_count=block_in.shape[-1],
        preferred_element_type=jnp.float32,
    )[0]


def owner_slots(bounds, owners, owner_id, slot_count, empty_row):
    lengths = bounds[1:] - bounds[:-1]
    mine = (owners == owner_id).astype(jnp.int32)
    taken = lengths * mine
    offsets = jnp.cumsum(taken) - taken
    slot_ids = jnp.arange(slot_count, dtype=jnp.int32)[:, None]
    hits = (
        (mine[None, :] > 0)
        & (slot_ids >= offsets[None, :])
        & (slot_ids < (offsets + lengths)[None, :])
    )
    found = jnp.sum(jnp.where(hits, bounds[:-1][None, :] + slot_ids - offsets[None, :], 0), axis=1)
    return jnp.where(jnp.any(hits, axis=1), found, empty_row)


def pass_forward(activation):
    return shifted(activation, "section", 1)


def pass_backward(gradient):
    return shifted(gradient, "section", -1)


def body(
    images,
    roster,
    cotangent,
    depth_kernel,
    up_weight,
    down_weight,
    layer_scale,
    master,
    first_moment,
    second_moment,
    bucket_bounds,
    bucket_owner,
):
    section_count = lax.axis_size("section")
    replica_count = lax.axis_size("dp")
    section_index = lax.axis_index("section")
    owner_index = lax.axis_index("dp")
    micro_count, height, breadth, channels = images.shape
    kernel = depth_kernel[0]
    up_matrix = up_weight[0]
    down_matrix = down_weight[0]
    scale_row = layer_scale[0]
    hidden_width = up_matrix.shape[1]
    positions = height * breadth
    slot_order = roster[0]
    blank_image = jnp.zeros((height, breadth, channels), jnp.bfloat16)

    def forward_slot(stash, slot, received):
        active = (slot >= 0) & (slot < micro_count)
        safe_slot = jnp.clip(slot, 0, micro_count - 1)
        first_input = images[slot_order[safe_slot]]
        block_in = jnp.where(section_index == 0, first_input, received)

        def forward_compute_slot(held):
            held_in, held_conv, held_pre, held_branch, held_out = held
            block_out, conv_rows, hidden_pre, branch = block_forward(
                block_in[None], kernel, up_matrix, down_matrix, scale_row
            )
            block_out = block_out[0]
            return (
                block_out,
                (
                    held_in.at[safe_slot].set(block_in),
                    held_conv.at[safe_slot].set(conv_rows),
                    held_pre.at[safe_slot].set(hidden_pre),
                    held_branch.at[safe_slot].set(branch),
                    held_out.at[safe_slot].set(block_out),
                ),
            )

        def forward_empty_slot(held):
            return (blank_image, held)

        return lax.cond(active, forward_compute_slot, forward_empty_slot, stash)

    def backward_slot(stash, totals, slot, received):
        active = (slot >= 0) & (slot < micro_count)
        safe_slot = jnp.clip(slot, 0, micro_count - 1)
        grad_out = jnp.where(section_index == section_count - 1, cotangent[safe_slot], received)
        held_in, held_conv, held_pre, held_branch, held_out = stash

        def backward_compute_slot(sums):
            kernel_sum, up_sum, down_sum, scale_sum = sums
            block_in = held_in[safe_slot]
            grad_in, scaled, hidden, grad_pre, normed, grad_conv, scale_terms = block_backward(
                grad_out[None],
                block_in[None],
                held_conv[safe_slot],
                held_pre[safe_slot],
                held_branch[safe_slot],
                kernel,
                up_matrix,
                down_matrix,
                scale_row,
            )
            kernel_sum = kernel_sum + kernel_grad(block_in, grad_conv[0], kernel)
            up_sum = up_sum + lax.dot_general(
                normed, grad_pre, (((0,), (0,)), ((), ())), preferred_element_type=jnp.float32
            )
            down_sum = down_sum + lax.dot_general(
                hidden, scaled, (((0,), (0,)), ((), ())), preferred_element_type=jnp.float32
            )
            scale_sum = scale_sum + jnp.sum(scale_terms, axis=0)
            return (grad_in[0], (kernel_sum, up_sum, down_sum, scale_sum))

        def backward_empty_slot(sums):
            return (blank_image, sums)

        return lax.cond(active, backward_compute_slot, backward_empty_slot, totals)

    stash = (
        jnp.zeros((micro_count, height, breadth, channels), jnp.bfloat16),
        jnp.zeros((micro_count, positions, channels), jnp.float32),
        jnp.zeros((micro_count, positions, hidden_width), jnp.float32),
        jnp.zeros((micro_count, positions, channels), jnp.float32),
        jnp.zeros((micro_count, height, breadth, channels), jnp.bfloat16),
    )
    totals = (
        jnp.zeros(kernel.shape, jnp.float32),
        jnp.zeros((channels, hidden_width), jnp.float32),
        jnp.zeros((hidden_width, channels), jnp.float32),
        jnp.zeros((channels,), jnp.float32),
    )

    def forward_tick(tick_index, loop_state):
        previous, held = loop_state
        received = pass_forward(previous)
        return forward_slot(held, tick_index - section_index, received)

    last_out, stash = lax.fori_loop(
        0, micro_count + section_count - 1, forward_tick, (blank_image, stash)
    )

    def backward_tick(tick_index, loop_state):
        previous, sums = loop_state
        received = pass_backward(previous)
        return backward_slot(
            stash, sums, tick_index - (section_count - 1 - section_index), received
        )

    last_grad, totals = lax.fori_loop(
        0, micro_count + section_count - 1, backward_tick, (blank_image, totals)
    )
    kernel_sum, up_sum, down_sum, scale_sum = totals
    flat_grad = jnp.concatenate(
        [kernel_sum.reshape(-1), up_sum.reshape(-1), down_sum.reshape(-1), scale_sum]
    ).astype(jnp.bfloat16)
    flat_grad = lax.optimization_barrier(flat_grad).astype(jnp.float32)
    row_count = flat_grad.shape[0] // GRAN
    owner_rows = -(-row_count // replica_count)
    unit_count = owner_rows * replica_count
    slot_count = master.shape[1]
    grad_rows = jnp.concatenate(
        [
            flat_grad.reshape(row_count, GRAN),
            jnp.zeros((unit_count - row_count + 1, GRAN), jnp.float32),
        ],
        axis=0,
    )
    bounds = bucket_bounds[0]
    owners = bucket_owner[0]
    summed = lax.psum(grad_rows[:unit_count].astype(jnp.bfloat16), "dp").astype(jnp.float32)
    summed = jnp.concatenate([summed, jnp.zeros((1, GRAN), jnp.float32)], axis=0)
    grad = summed[owner_slots(bounds, owners, owner_index, slot_count, unit_count)]
    grad = grad / replica_count
    new_first = beta_one * first_moment[0] + (1.0 - beta_one) * grad
    new_second = beta_two * second_moment[0] + (1.0 - beta_two) * grad * grad
    update = (
        new_first / first_fix / (jnp.sqrt(new_second / second_fix) + adam_eps)
        + decay_rate * master[0]
    )
    new_master = master[0] - learn_rate * update
    return (stash[4][None], new_master[None], new_first[None], new_second[None])


def solution(mesh):
    placed = (
        P("dp", None, None, None),
        P("dp", None),
        P("dp", None, None, None),
        P("section", None, None, None),
        P("section", None, None),
        P("section", None, None),
        P("section", None),
        P("section", "dp", None),
        P("section", "dp", None),
        P("section", "dp", None),
        P("section", None),
        P("section", None),
    )
    return jax.shard_map(
        body,
        mesh=mesh,
        in_specs=placed,
        out_specs=(
            P("section", "dp", None, None, None),
            P("section", "dp", None),
            P("section", "dp", None),
            P("section", "dp", None),
        ),
        check_vma=False,
    )
```

profile of v0, /device:TPU:0, one launch (start us, length us, event | category | flops | bytes accessed | tf_op | source)
XLA Modules:
  0.0 925.9 jit_solution(11362853815974126616)
XLA Ops:
  14.6 178.7 %while.52 = (s32[]{:T(128)}, bf16[16,16,768]{2,1,0:T(8,128)(2,1)}, bf16[2,16,16,768]{3,2,1,0:T(8,128)(2,1)}, f32[2,256,768]{2,1,0:T(8,128)S(1)}, f32[2,256,3072]...) while((s32[]{:T(128)}, bf16[16,16,768]{2,1,0:T(8,128)(2,1)}, ...), condition=%wide.region_7.0_spmd, body=%wide.region_0.7_spmd.sunk | while | flops 2486329600 | bytes 55546536 | solution.py:238
  19.5 8.6 collective-permute-done
  28.1 40.8 %conditional.4 = (bf16[16,16,768]{2,1,0:T(8,128)(2,1)}, bf16[2,16,16,768]{3,2,1,0:T(8,128)(2,1)}, f32[2,256,768]{2,1,0:T(8,128)S(1)}, f32[2,256,3072]{2,1,0:T(8,...) conditional(s32[]{:T(128)} %convert_element_type.138, (bf16[2,16,16,768]{3,2,1,0:T(8,128)(2,1)}, ...), branch_computations={%region_1.1_spmd, %region_2.6_spmd} | conditional | flops 2486329600 | bytes 53973268 | solution.py:182
  36.6 8.6 fusion.152
  47.2 7.7 fusion.3
  54.9 8.6 fusion.15
  70.2 8.0 collective-permute-done
  78.3 40.8 %conditional.4 = (bf16[16,16,768]{2,1,0:T(8,128)(2,1)}, bf16[2,16,16,768]{3,2,1,0:T(8,128)(2,1)}, f32[2,256,768]{2,1,0:T(8,128)S(1)}, f32[2,256,3072]{2,1,0:T(8,...) conditional(s32[]{:T(128)} %convert_element_type.138, (bf16[2,16,16,768]{3,2,1,0:T(8,128)(2,1)}, ...), branch_computations={%region_1.1_spmd, %region_2.6_spmd} | conditional | flops 2486329600 | bytes 53973268 | solution.py:182
  86.8 8.6 fusion.152
  97.4 7.7 fusion.3
  105.0 8.6 fusion.15
  131.3 44.3 %collective-permute-start = (bf16[16,16,768]{2,1,0:T(8,128)(2,1)}, bf16[16,16,768]{2,1,0:T(8,128)(2,1)S(1)}, u32[]{:S(2)}, u32[]{:S(2)}) collective-permute-start(bf16[16,16,768]{2,1,0:T(8,128)(2,1)} %get-tuple-element.1440), channel_id=1, source_target_pairs={{0,8},{8,16},{16,24},{1,9},{9,17},{17,25},{2,10},{10,18},{18,26},{... | collective-permute-start | bytes 1179656 | tf_op jit(solution)/shard_map/while/body/eval_jaxpr/ppermute | solution.py:22
  203.7 363.9 %while.53 = (s32[]{:T(128)}, bf16[16,16,768]{2,1,0:T(8,128)(2,1)}, f32[7,7,768]{2,1,0:T(8,128)S(1)}, f32[768,3072]{1,0:T(8,128)}, f32[3072,768]{1,0:T(8,128)}, /...) while((s32[]{:T(128)}, bf16[16,16,768]{2,1,0:T(8,128)(2,1)}, ...), condition=%wide.region_16.0_spmd, body=%wide.region_8.16_spmd.sunk | while | flops 4936299520 | bytes 245418480 | solution.py:249
  216.3 49.0 %collective-permute-done.1 = bf16[16,16,768]{2,1,0:T(8,128)(2,1)S(1)} collective-permute-done((bf16[16,16,768]{2,1,0:T(8,128)(2,1)}, bf16[16,16,768]{2,1,0:T(8,128)(2,1)S(1)}, u32[]{:S(2)}, u32[]{:S(2)}) %collective-permute-start.1) | collective-permute-done | bytes 393248 | tf_op jit(solution)/shard_map/while/body/eval_jaxpr/ppermute | solution.py:22
  267.3 9.8 %collective-permute-done.1 = bf16[16,16,768]{2,1,0:T(8,128)(2,1)S(1)} collective-permute-done((bf16[16,16,768]{2,1,0:T(8,128)(2,1)}, bf16[16,16,768]{2,1,0:T(8,128)(2,1)S(1)}, u32[]{:S(2)}, u32[]{:S(2)}) %collective-permute-start.1) | collective-permute-done | bytes 393248 | tf_op jit(solution)/shard_map/while/body/eval_jaxpr/ppermute | solution.py:22
  279.2 45.3 %collective-permute-done.1 = bf16[16,16,768]{2,1,0:T(8,128)(2,1)S(1)} collective-permute-done((bf16[16,16,768]{2,1,0:T(8,128)(2,1)}, bf16[16,16,768]{2,1,0:T(8,128)(2,1)S(1)}, u32[]{:S(2)}, u32[]{:S(2)}) %collective-permute-start.1) | collective-permute-done | bytes 393248 | tf_op jit(solution)/shard_map/while/body/eval_jaxpr/ppermute | solution.py:22
  326.6 139.2 %collective-permute-done.1 = bf16[16,16,768]{2,1,0:T(8,128)(2,1)S(1)} collective-permute-done((bf16[16,16,768]{2,1,0:T(8,128)(2,1)}, bf16[16,16,768]{2,1,0:T(8,128)(2,1)S(1)}, u32[]{:S(2)}, u32[]{:S(2)}) %collective-permute-start.1) | collective-permute-done | bytes 393248 | tf_op jit(solution)/shard_map/while/body/eval_jaxpr/ppermute | solution.py:22
  465.8 45.3 %conditional.5 = (bf16[16,16,768]{2,1,0:T(8,128)(2,1)}, f32[7,7,768]{2,1,0:T(8,128)S(1)}, f32[768,3072]{1,0:T(8,128)}, f32[3072,768]{1,0:T(8,128)}, f32[768]{0:T(1024)}) conditional(s32[]{:T(128)} %convert_element_type.139, (f32[7,7,768]{2,1,0:T(8,128)S(1)}, f32[768,3072]{1,0:T(8,128)}, f32[3072,768]{1,0:T(8,128)}, f32[768]{0:T(1024)}) %tuple.137, ...), branch_computations={%region_9.9_spmd, %region_10.15_spmd} | conditional | flops 4936299520 | bytes 243845184 | solution.py:217
  489.4 7.3 fusion.100
  499.1 8.3 convolution_add_fusion
  512.4 9.5 %collective-permute-done.1 = bf16[16,16,768]{2,1,0:T(8,128)(2,1)S(1)} collective-permute-done((bf16[16,16,768]{2,1,0:T(8,128)(2,1)}, bf16[16,16,768]{2,1,0:T(8,128)(2,1)S(1)}, u32[]{:S(2)}, u32[]{:S(2)}) %collective-permute-start.1) | collective-permute-done | bytes 393248 | tf_op jit(solution)/shard_map/while/body/eval_jaxpr/ppermute | solution.py:22
  521.9 45.3 %conditional.5 = (bf16[16,16,768]{2,1,0:T(8,128)(2,1)}, f32[7,7,768]{2,1,0:T(8,128)S(1)}, f32[768,3072]{1,0:T(8,128)}, f32[3072,768]{1,0:T(8,128)}, f32[768]{0:T(1024)}) conditional(s32[]{:T(128)} %convert_element_type.139, (f32[7,7,768]{2,1,0:T(8,128)S(1)}, f32[768,3072]{1,0:T(8,128)}, f32[3072,768]{1,0:T(8,128)}, f32[768]{0:T(1024)}) %tuple.137, ...), branch_computations={%region_9.9_spmd, %region_10.15_spmd} | conditional | flops 4936299520 | bytes 243845184 | solution.py:217
  545.5 7.3 fusion.100
  555.2 8.3 convolution_add_fusion
  574.6 9.2 reshape.381
  592.2 16.7 %pad_maximum_fusion = bf16[4756992]{0:T(1024)(128)(2,1)S(1)} fusion(bf16[768]{0:T(1024)(128)(2,1)S(1)} %convert.26, bf16[2359296]{0:T(1024)(128)(2,1)} %reshape.381, bf16[2359296]{0:T(1024)(128)(2,1)} %bitcast.124, bf16[37632]{0:T(1024)(128)(2,1)S(1)} %reshape.379), kind=kLoop, calls=%fused_computation.200 | loop fusion | flops 38055936 | bytes 19027968 | tf_op jit(solution)/shard_map/concatenate | solution.py:253
  616.9 195.2 %all-reduce.5.cloned.1.call-done = bf16[37168,128]{1,0:T(8,128)(2,1)} async-done(((bf16[37168,128]{1,0:T(8,128)(2,1)}), bf16[37168,128]{1,0:T(8,128)(2,1)}) %all-reduce.5.cloned.1.call-update) | async-done | bytes 9515024 | tf_op jit(solution)/shard_map/psum | solution.py:270
  812.1 10.9 %pad_convert_fusion = f32[37169,128]{1,0:T(8,128)} fusion(bf16[37168,128]{1,0:T(8,128)(2,1)} %all-reduce.5.cloned.1.call-done), kind=kLoop, calls=%fused_computation.198 | loop fusion | flops 4757632 | bytes 28545536 | tf_op jit(solution)/shard_map/concatenate | solution.py:271
  823.0 20.4 %gather_fusion = f32[6969,128]{1,0:T(8,128)} fusion(f32[37169,128]{1,0:T(8,128)} %pad_convert_fusion, s32[7168]{0:T(1024)S(1)} %pad_clamp_fusion), kind=kCustom, calls=%fused_computation | custom fusion | bytes 7164132 | tf_op jit(solution)/shard_map/gather | solution.py:272
  850.0 23.1 %copy.56 = f32[1,6969,128]{2,0,1:T(1,128)} copy(f32[1,6969,128]{2,1,0:T(8,128)S(1)} %get-tuple-element.1165) | data formatting | bytes 7136256
  873.1 22.9 %copy.57 = f32[1,6969,128]{2,0,1:T(1,128)} copy(f32[1,6969,128]{2,1,0:T(8,128)S(1)} %get-tuple-element.1166) | data formatting | bytes 7136256
  896.0 22.9 %copy.58 = f32[1,6969,128]{2,0,1:T(1,128)} copy(f32[1,6969,128]{2,1,0:T(8,128)S(1)} %get-tuple-element.1167) | data formatting | bytes 7136256
  (220 shorter events, 183.5 us)
Async XLA Ops:
  7.2 804.9 %all-reduce.5.cloned.1.call-start = ((), (), s32[]{:S(2)}) async-start(), calls=%async_computation | async-start | bytes 19030016 | tf_op jit(solution)/shard_map/psum | solution.py:270
  14.6 13.5 %collective-permute-start = (bf16[16,16,768]{2,1,0:T(8,128)(2,1)}, bf16[16,16,768]{2,1,0:T(8,128)(2,1)S(1)}, u32[]{:S(2)}, u32[]{:S(2)}) collective-permute-start(bf16[16,16,768]{2,1,0:T(8,128)(2,1)} %get-tuple-element.1440), channel_id=1, source_target_pairs={{0,8},{8,16},{16,24},{1,9},{9,17},{17,25},{2,10},{10,18},{18,26},{... | collective-permute-start | bytes 1179656 | tf_op jit(solution)/shard_map/while/body/eval_jaxpr/ppermute | solution.py:22
  34.6 10.7 %copy-start.2 = (bf16[16,16,768]{2,1,0:T(8,128)(2,1)}, bf16[16,16,768]{2,1,0:T(8,128)(2,1)S(1)}, u32[]{:S(2)}) copy-start(bf16[16,16,768]{2,1,0:T(8,128)(2,1)S(1)} %get-tuple-element.1162) | copy-start | bytes 1179652 | tf_op jit(solution)/shard_map/while/body/eval_jaxpr/cond
  47.0 7.9 slice-start.10
  47.2 7.7 copy-start.3
  47.2 7.7 slice-start.11
  68.9 9.4 %collective-permute-start = (bf16[16,16,768]{2,1,0:T(8,128)(2,1)}, bf16[16,16,768]{2,1,0:T(8,128)(2,1)S(1)}, u32[]{:S(2)}, u32[]{:S(2)}) collective-permute-start(bf16[16,16,768]{2,1,0:T(8,128)(2,1)} %get-tuple-element.1440), channel_id=1, source_target_pairs={{0,8},{8,16},{16,24},{1,9},{9,17},{17,25},{2,10},{10,18},{18,26},{... | collective-permute-start | bytes 1179656 | tf_op jit(solution)/shard_map/while/body/eval_jaxpr/ppermute | solution.py:22
  84.7 10.7 %copy-start.2 = (bf16[16,16,768]{2,1,0:T(8,128)(2,1)}, bf16[16,16,768]{2,1,0:T(8,128)(2,1)S(1)}, u32[]{:S(2)}) copy-start(bf16[16,16,768]{2,1,0:T(8,128)(2,1)S(1)} %get-tuple-element.1162) | copy-start | bytes 1179652 | tf_op jit(solution)/shard_map/while/body/eval_jaxpr/cond
  97.2 7.9 slice-start.10
  97.3 7.7 copy-start.3
  97.3 7.7 slice-start.11
  119.1 11.4 %collective-permute-start = (bf16[16,16,768]{2,1,0:T(8,128)(2,1)}, bf16[16,16,768]{2,1,0:T(8,128)(2,1)S(1)}, u32[]{:S(2)}, u32[]{:S(2)}) collective-permute-start(bf16[16,16,768]{2,1,0:T(8,128)(2,1)} %get-tuple-element.1440), channel_id=1, source_target_pairs={{0,8},{8,16},{16,24},{1,9},{9,17},{17,25},{2,10},{10,18},{18,26},{... | collective-permute-start | bytes 1179656 | tf_op jit(solution)/shard_map/while/body/eval_jaxpr/ppermute | solution.py:22
  131.3 50.5 %collective-permute-start = (bf16[16,16,768]{2,1,0:T(8,128)(2,1)}, bf16[16,16,768]{2,1,0:T(8,128)(2,1)S(1)}, u32[]{:S(2)}, u32[]{:S(2)}) collective-permute-start(bf16[16,16,768]{2,1,0:T(8,128)(2,1)} %get-tuple-element.1440), channel_id=1, source_target_pairs={{0,8},{8,16},{16,24},{1,9},{9,17},{17,25},{2,10},{10,18},{18,26},{... | collective-permute-start | bytes 1179656 | tf_op jit(solution)/shard_map/while/body/eval_jaxpr/ppermute | solution.py:22
  182.6 9.9 %collective-permute-start = (bf16[16,16,768]{2,1,0:T(8,128)(2,1)}, bf16[16,16,768]{2,1,0:T(8,128)(2,1)S(1)}, u32[]{:S(2)}, u32[]{:S(2)}) collective-permute-start(bf16[16,16,768]{2,1,0:T(8,128)(2,1)} %get-tuple-element.1440), channel_id=1, source_target_pairs={{0,8},{8,16},{16,24},{1,9},{9,17},{17,25},{2,10},{10,18},{18,26},{... | collective-permute-start | bytes 1179656 | tf_op jit(solution)/shard_map/while/body/eval_jaxpr/ppermute | solution.py:22
  214.9 50.3 %collective-permute-start.1 = (bf16[16,16,768]{2,1,0:T(8,128)(2,1)}, bf16[16,16,768]{2,1,0:T(8,128)(2,1)S(1)}, u32[]{:S(2)}, u32[]{:S(2)}) collective-permute-start(bf16[16,16,768]{2,1,0:T(8,128)(2,1)} %get-tuple-element.1496), channel_id=1, source_target_pairs={{8,0},{16,8},{24,16},{9,1},{17,9},{25,17},{10,2},{18,10},{26,18},{... | collective-permute-start | bytes 1179656 | tf_op jit(solution)/shard_map/while/body/eval_jaxpr/ppermute | solution.py:22
  266.0 11.1 %collective-permute-start.1 = (bf16[16,16,768]{2,1,0:T(8,128)(2,1)}, bf16[16,16,768]{2,1,0:T(8,128)(2,1)S(1)}, u32[]{:S(2)}, u32[]{:S(2)}) collective-permute-start(bf16[16,16,768]{2,1,0:T(8,128)(2,1)} %get-tuple-element.1496), channel_id=1, source_target_pairs={{8,0},{16,8},{24,16},{9,1},{17,9},{25,17},{10,2},{18,10},{26,18},{... | collective-permute-start | bytes 1179656 | tf_op jit(solution)/shard_map/while/body/eval_jaxpr/ppermute | solution.py:22
  277.9 46.6 %collective-permute-start.1 = (bf16[16,16,768]{2,1,0:T(8,128)(2,1)}, bf16[16,16,768]{2,1,0:T(8,128)(2,1)S(1)}, u32[]{:S(2)}, u32[]{:S(2)}) collective-permute-start(bf16[16,16,768]{2,1,0:T(8,128)(2,1)} %get-tuple-element.1496), channel_id=1, source_target_pairs={{8,0},{16,8},{24,16},{9,1},{17,9},{25,17},{10,2},{18,10},{26,18},{... | collective-permute-start | bytes 1179656 | tf_op jit(solution)/shard_map/while/body/eval_jaxpr/ppermute | solution.py:22
  325.3 140.5 %collective-permute-start.1 = (bf16[16,16,768]{2,1,0:T(8,128)(2,1)}, bf16[16,16,768]{2,1,0:T(8,128)(2,1)S(1)}, u32[]{:S(2)}, u32[]{:S(2)}) collective-permute-start(bf16[16,16,768]{2,1,0:T(8,128)(2,1)} %get-tuple-element.1496), channel_id=1, source_target_pairs={{8,0},{16,8},{24,16},{9,1},{17,9},{25,17},{10,2},{18,10},{26,18},{... | collective-permute-start | bytes 1179656 | tf_op jit(solution)/shard_map/while/body/eval_jaxpr/ppermute | solution.py:22
  488.0 11.0 %slice-start.5 = ((s8[6291456]{0:T(1024)(128)(4,1)}), s8[4194304]{0:T(1024)(128)(4,1)S(1)}, s32[]{:S(2)}) async-start(s8[6291456]{0:T(1024)(128)(4,1)} %bitcast.119), calls=%async_computation.6 | async-start | bytes 8388608 | tf_op jit(solution)/shard_map/while/body/eval_jaxpr/cond
  489.4 7.5 slice-start
  489.4 9.7 %slice-start.6 = ((s8[6291456]{0:T(1024)(128)(4,1)}), s8[2097152]{0:T(1024)(128)(4,1)S(1)}, s32[]{:S(2)}) async-start(s8[6291456]{0:T(1024)(128)(4,1)} %bitcast.119), calls=%async_computation.7 | async-start | bytes 4194304 | tf_op jit(solution)/shard_map/while/body/eval_jaxpr/cond
  489.4 9.7 %slice-start.7 = ((s8[9437184]{0:T(1024)(128)(4,1)}), s8[4194304]{0:T(1024)(128)(4,1)S(1)}, s32[]{:S(2)}) async-start(s8[9437184]{0:T(1024)(128)(4,1)} %bitcast.122), calls=%async_computation.8 | async-start | bytes 8388608 | tf_op jit(solution)/shard_map/while/body/eval_jaxpr/cond
  489.4 9.7 %slice-start.8 = ((s8[9437184]{0:T(1024)(128)(4,1)}), s8[4194304]{0:T(1024)(128)(4,1)S(1)}, s32[]{:S(2)}) async-start(s8[9437184]{0:T(1024)(128)(4,1)} %bitcast.122), calls=%async_computation.9 | async-start | bytes 8388608 | tf_op jit(solution)/shard_map/while/body/eval_jaxpr/cond
  499.1 8.4 copy-start
  499.1 12.0 %copy-start.8 = (f32[7,7,768]{2,1,0:T(8,128)S(1)}, f32[7,7,768]{2,1,0:T(8,128)}, u32[]{:S(2)}) copy-start(f32[7,7,768]{2,1,0:T(8,128)} %copy-done.7) | copy-start | bytes 451588 | tf_op jit(solution)/shard_map/while/body/eval_jaxpr/cond
  511.1 10.8 %collective-permute-start.1 = (bf16[16,16,768]{2,1,0:T(8,128)(2,1)}, bf16[16,16,768]{2,1,0:T(8,128)(2,1)S(1)}, u32[]{:S(2)}, u32[]{:S(2)}) collective-permute-start(bf16[16,16,768]{2,1,0:T(8,128)(2,1)} %get-tuple-element.1496), channel_id=1, source_target_pairs={{8,0},{16,8},{24,16},{9,1},{17,9},{25,17},{10,2},{18,10},{26,18},{... | collective-permute-start | bytes 1179656 | tf_op jit(solution)/shard_map/while/body/eval_jaxpr/ppermute | solution.py:22
  544.1 11.0 %slice-start.5 = ((s8[6291456]{0:T(1024)(128)(4,1)}), s8[4194304]{0:T(1024)(128)(4,1)S(1)}, s32[]{:S(2)}) async-start(s8[6291456]{0:T(1024)(128)(4,1)} %bitcast.119), calls=%async_computation.6 | async-start | bytes 8388608 | tf_op jit(solution)/shard_map/while/body/eval_jaxpr/cond
  545.5 9.7 %slice-start.6 = ((s8[6291456]{0:T(1024)(128)(4,1)}), s8[2097152]{0:T(1024)(128)(4,1)S(1)}, s32[]{:S(2)}) async-start(s8[6291456]{0:T(1024)(128)(4,1)} %bitcast.119), calls=%async_computation.7 | async-start | bytes 4194304 | tf_op jit(solution)/shard_map/while/body/eval_jaxpr/cond
  545.5 9.7 %slice-start.7 = ((s8[9437184]{0:T(1024)(128)(4,1)}), s8[4194304]{0:T(1024)(128)(4,1)S(1)}, s32[]{:S(2)}) async-start(s8[9437184]{0:T(1024)(128)(4,1)} %bitcast.122), calls=%async_computation.8 | async-start | bytes 8388608 | tf_op jit(solution)/shard_map/while/body/eval_jaxpr/cond
  545.5 9.7 %slice-start.8 = ((s8[9437184]{0:T(1024)(128)(4,1)}), s8[4194304]{0:T(1024)(128)(4,1)S(1)}, s32[]{:S(2)}) async-start(s8[9437184]{0:T(1024)(128)(4,1)} %bitcast.122), calls=%async_computation.9 | async-start | bytes 8388608 | tf_op jit(solution)/shard_map/while/body/eval_jaxpr/cond
  555.1 8.4 copy-start
  555.2 12.0 %copy-start.8 = (f32[7,7,768]{2,1,0:T(8,128)S(1)}, f32[7,7,768]{2,1,0:T(8,128)}, u32[]{:S(2)}) copy-start(f32[7,7,768]{2,1,0:T(8,128)} %copy-done.7) | copy-start | bytes 451588 | tf_op jit(solution)/shard_map/while/body/eval_jaxpr/cond
  (24 other events, 106.7 us)
Sparse Core Ops, SparseCore 0:
  615.2 196.8 all-reduce.4
where the time goes:
time: 933 us; the launch traced here: 926 us
  waiting for transfers between devices  484 us (52%)
  local copies, waits for them, and re-layouts  148 us (16%)
  matrix products  113 us (12%)
  other arithmetic  85.3 us (9%)
  starting transfers between devices  65.5 us (7%)
  loops' own time  16.6 us (2%)
  between operations  14.3 us (2%)
    ppermute x10, waiting for transfers between devices, shifted(): return lax.ppermute(block, axis, route)  288 us
    psum x1, waiting for transfers between devices, body(): lax.psum(grad_rows[:unit_count].astype(jnp.bfloat16), 'dp')  195 us
    unnamed x10, local copies, waits for them, and re-layouts  73.1 us
    ppermute x10, starting transfers between devices, shifted(): return lax.ppermute(block, axis, route)  65.5 us
    conv_general_dilated x4, matrix products, depthwise(): lax.conv_general_dilated(inputs, kernel[:, :, None, :], (1, 1), ((reach,...  28.9 us
    gather x1, local copies, waits for them, and re-layouts, body(): summed[owner_slots(bounds, owners, owner_index, slot_count, unit_count)]  20.4 us
  transfers between devices with their start and end apart: 11, of which 11 were waited for; matrix products, arithmetic and copies ran while one was open for 0% of the time, Pallas kernels for 0%

commit v1 on v0

v1 whole, which is shorter than its diff:
```python
import functools

import jax
import jax.numpy as jnp
from jax import lax
from jax.experimental import pallas as pl
from jax.experimental.pallas import tpu as pltpu
from jax.sharding import PartitionSpec as P

GRAN = 128


beta_one = 0.9
beta_two = 0.95
learn_rate = 0.01
decay_rate = 0.1
adam_eps = 1e-08
norm_eps = 1e-06
first_fix = 1.0 - 0.9**10
second_fix = 1.0 - 0.95**10


def shifted(block, axis, distance):
    devices = range(lax.axis_size(axis))
    route = [(i - distance, i) for i in devices if i - distance in devices]
    return lax.ppermute(block, axis, route)


def depthwise(inputs, kernel):
    reach = (kernel.shape[0] - 1) // 2
    return lax.conv_general_dilated(
        inputs,
        kernel[:, :, None, :],
        (1, 1),
        ((reach, reach), (reach, reach)),
        dimension_numbers=("NHWC", "HWIO", "NHWC"),
        feature_group_count=inputs.shape[-1],
        preferred_element_type=jnp.float32,
    )


def gelu_slope(values):
    cumulative = 0.5 * (1.0 + lax.erf(values * 0.7071067811865476))
    return cumulative + values * jnp.exp(-0.5 * values * values) * 0.3989422804014327


def normalize(conv_rows):
    centred = conv_rows - jnp.mean(conv_rows, axis=-1, keepdims=True)
    inv_std = lax.rsqrt(jnp.mean(centred * centred, axis=-1, keepdims=True) + norm_eps)
    return (centred * inv_std, inv_std)


def block_forward(block_in, kernel, up_matrix, down_matrix, scale_row):
    channels = block_in.shape[-1]
    conv_rows = depthwise(block_in, kernel).reshape(-1, channels)
    normed_f, inv_std = normalize(conv_rows)
    normed = normed_f.astype(jnp.bfloat16)
    hidden_pre = jnp.dot(normed, up_matrix, preferred_element_type=jnp.float32)
    hidden = jax.nn.gelu(hidden_pre, approximate=False).astype(jnp.bfloat16)
    branch = jnp.dot(hidden, down_matrix, preferred_element_type=jnp.float32)
    block_out = block_in.reshape(-1, channels).astype(jnp.float32) + scale_row * branch
    return (block_out.astype(jnp.bfloat16).reshape(block_in.shape), conv_rows, hidden_pre, branch)


def block_backward(
    grad_out, conv_rows, hidden_pre, kernel, up_matrix, down_matrix, scale_row
):
    channels = grad_out.shape[-1]
    out_rows = grad_out.reshape(-1, channels).astype(jnp.float32)
    scaled = (out_rows * scale_row).astype(jnp.bfloat16)
    grad_hidden = lax.dot_general(
        scaled, down_matrix, (((1,), (1,)), ((), ())), preferred_element_type=jnp.float32
    )
    grad_pre = (grad_hidden * gelu_slope(hidden_pre)).astype(jnp.bfloat16)
    normed_f, inv_std = normalize(conv_rows)
    grad_normed = lax.dot_general(
        grad_pre, up_matrix, (((1,), (1,)), ((), ())), preferred_element_type=jnp.float32
    )
    grad_conv = inv_std * (
        grad_normed
        - jnp.mean(grad_normed, axis=-1, keepdims=True)
        - normed_f * jnp.mean(grad_normed * normed_f, axis=-1, keepdims=True)
    )
    grad_conv = grad_conv.astype(jnp.bfloat16).reshape(grad_out.shape)
    back_conv = depthwise(grad_conv, kernel[::-1, ::-1])
    grad_in = (
        (out_rows + back_conv.reshape(-1, channels)).astype(jnp.bfloat16).reshape(grad_out.shape)
    )
    return (grad_in, grad_pre, grad_conv)


def kernel_grad(block_in, grad_conv, kernel):
    reach = (kernel.shape[0] - 1) // 2
    padded = jnp.pad(block_in, ((reach, reach), (reach, reach), (0, 0)))
    return lax.conv_general_dilated(
        padded[None],
        grad_conv[:, :, None, :],
        (1, 1),
        ((0, 0), (0, 0)),
        dimension_numbers=("NHWC", "HWIO", "NHWC"),
        feature_group_count=block_in.shape[-1],
        preferred_element_type=jnp.float32,
    )[0]


def spread_kernel(step, bounds, owners, *refs):
    *part_refs, spread_ref, rows_ref, gathered = refs
    owner_id = pl.program_id(0)

    @pl.when(owner_id == 0)
    def lay_out():
        base = 0
        for part_ref in part_refs:
            count = part_ref.shape[0]

            def copy(index, carry, part_ref=part_ref, base=base):
                first = pl.multiple_of(index * step, step)
                rows_ref[pl.ds(base + first, step), :] = part_ref[pl.ds(first, step), :]
                return carry

            whole = count // step * step
            lax.fori_loop(0, whole // step, copy, 0)
            if whole < count:
                rows_ref[base + whole : base + count, :] = part_ref[whole:count, :]
            base += count
        rows_ref[base:, :] = jnp.zeros((rows_ref.shape[0] - base, GRAN), jnp.float32)

    def bucket(index, filled):
        start = bounds[index]
        length = jnp.where(owners[index] == owner_id, bounds[index + 1] - start, 0)

        def chunk(part, carry):
            gathered[pl.ds(filled + part * step, step), :] = rows_ref[
                pl.ds(start + part * step, step), :
            ]
            return carry

        lax.fori_loop(0, (length + step - 1) // step, chunk, 0)
        return filled + length

    filled = lax.fori_loop(0, owners.shape[0], bucket, 0)

    def finish(part, carry):
        first = pl.multiple_of(part * 16, 16)
        ids = first + lax.broadcasted_iota(jnp.int32, (16, GRAN), 0)
        kept = jnp.where(ids < filled, gathered[pl.ds(first, 16), :], 0.0)
        spread_ref[0, pl.ds(first, 16), :] = kept.astype(spread_ref.dtype)
        return carry

    lax.fori_loop(0, spread_ref.shape[1] // 16, finish, 0, unroll=4)


def spread_rows(parts, bounds, owners, owner_count, unit_count, slot_rows, step):
    return pl.pallas_call(
        functools.partial(spread_kernel, step),
        out_shape=jax.ShapeDtypeStruct((owner_count, slot_rows, GRAN), jnp.bfloat16),
        grid_spec=pltpu.PrefetchScalarGridSpec(
            num_scalar_prefetch=2,
            grid=(owner_count,),
            in_specs=[pl.BlockSpec(memory_space=pltpu.VMEM)] * len(parts),
            out_specs=pl.BlockSpec((1, slot_rows, GRAN), lambda d, *_: (d, 0, 0)),
            scratch_shapes=[
                pltpu.VMEM((unit_count + step, GRAN), jnp.float32),
                pltpu.VMEM((slot_rows + step, GRAN), jnp.float32),
            ],
        ),
        compiler_params=pltpu.CompilerParams(vmem_limit_bytes=56 * 2**20),
        name="spread_rows",
    )(bounds, owners, *parts)


def adam_kernel(part, count, grad_ref, master_ref, first_ref, second_ref, *outs):
    def chunk(index, carry):
        where = pl.ds(pl.multiple_of(index * part, part), part)
        grad = grad_ref[where, :].astype(jnp.float32) / count
        master = master_ref[where, 0, :]
        new_first = beta_one * first_ref[where, 0, :] + (1.0 - beta_one) * grad
        new_second = beta_two * second_ref[where, 0, :] + (1.0 - beta_two) * grad * grad
        update = (
            new_first / first_fix / (jnp.sqrt(new_second / second_fix) + adam_eps)
            + decay_rate * master
        )
        outs[0][where, 0, :] = master - learn_rate * update
        outs[1][where, 0, :] = new_first
        outs[2][where, 0, :] = new_second
        return carry

    lax.fori_loop(0, grad_ref.shape[0] // part, chunk, 0)


def adam(grad, master, first, second, count):
    block, part = 512, 64
    slots = master.shape[1]
    state = pl.BlockSpec((block, 1, GRAN), lambda i: (i, 0, 0))
    shape = jax.ShapeDtypeStruct((slots, 1, GRAN), jnp.float32)
    results = pl.pallas_call(
        functools.partial(adam_kernel, part, count),
        out_shape=(shape,) * 3,
        grid=(pl.cdiv(slots, block),),
        in_specs=[pl.BlockSpec((block, GRAN), lambda i: (i, 0)), state, state, state],
        out_specs=(state,) * 3,
        name="adam",
    )(grad, *(jnp.swapaxes(held, 0, 1) for held in (master, first, second)))
    return [jnp.swapaxes(held, 0, 1) for held in results]


def pass_forward(activation):
    return shifted(activation, "section", 1)


def pass_backward(gradient):
    return shifted(gradient, "section", -1)


def body(
    images,
    roster,
    cotangent,
    depth_kernel,
    up_weight,
    down_weight,
    layer_scale,
    master,
    first_moment,
    second_moment,
    bucket_bounds,
    bucket_owner,
):
    section_count = lax.axis_size("section")
    replica_count = lax.axis_size("dp")
    section_index = lax.axis_index("section")
    micro_count, height, breadth, channels = images.shape
    kernel = depth_kernel[0]
    up_matrix = up_weight[0]
    down_matrix = down_weight[0]
    scale_row = layer_scale[0]
    hidden_width = up_matrix.shape[1]
    positions = height * breadth
    slot_order = roster[0]
    tick_count = micro_count + section_count - 1

    held_in = jnp.zeros((micro_count + 1, height, breadth, channels), jnp.bfloat16)
    held_conv = jnp.zeros((micro_count + 1, positions, channels), jnp.float32)
    held_pre = jnp.zeros((micro_count + 1, positions, hidden_width), jnp.float32)
    held_branch = jnp.zeros((micro_count + 1, positions, channels), jnp.float32)
    held_out = jnp.zeros((micro_count + 1, height, breadth, channels), jnp.bfloat16)

    def slot_and_place(slot):
        safe_slot = jnp.clip(slot, 0, micro_count - 1)
        return safe_slot, jnp.where(slot == safe_slot, slot, micro_count)

    block_out = None
    for tick in range(tick_count):
        safe_slot, place = slot_and_place(tick - section_index)
        block_in = images[slot_order[safe_slot]]
        if tick > 0:
            block_in = jnp.where(section_index == 0, block_in, pass_forward(block_out))
        block_out, conv_rows, hidden_pre, branch = block_forward(
            block_in[None], kernel, up_matrix, down_matrix, scale_row
        )
        block_out = block_out[0]
        held_in = held_in.at[place].set(block_in)
        held_conv = held_conv.at[place].set(conv_rows)
        held_pre = held_pre.at[place].set(hidden_pre)
        held_branch = held_branch.at[place].set(branch)
        held_out = held_out.at[place].set(block_out)

    slot_in = held_in[:micro_count]
    slot_conv = held_conv[:micro_count]
    slot_pre = held_pre[:micro_count]
    slot_branch = held_branch[:micro_count]
    slot_out = held_out[:micro_count]

    held_grad = jnp.zeros((micro_count + 1, height, breadth, channels), jnp.bfloat16)
    held_grad_pre = jnp.zeros((micro_count + 1, positions, hidden_width), jnp.bfloat16)
    held_grad_conv = jnp.zeros((micro_count + 1, height, breadth, channels), jnp.bfloat16)
    steps_after = section_count - 1 - section_index
    grad_in = None
    for tick in range(tick_count):
        safe_slot, place = slot_and_place(tick - steps_after)
        grad_out = cotangent[safe_slot]
        if tick > 0:
            grad_out = jnp.where(steps_after == 0, grad_out, pass_backward(grad_in))
        grad_in, grad_pre, grad_conv = block_backward(
            grad_out[None],
            slot_conv[safe_slot],
            slot_pre[safe_slot],
            kernel,
            up_matrix,
            down_matrix,
            scale_row,
        )
        grad_in = grad_in[0]
        held_grad = held_grad.at[place].set(grad_out)
        held_grad_pre = held_grad_pre.at[place].set(grad_pre)
        held_grad_conv = held_grad_conv.at[place].set(grad_conv[0])

    out_rows = held_grad[:micro_count].reshape(-1, channels).astype(jnp.float32)
    grad_pre = held_grad_pre[:micro_count].reshape(-1, hidden_width)
    grad_conv = held_grad_conv[:micro_count]
    scaled = (out_rows * scale_row).astype(jnp.bfloat16)
    hidden = jax.nn.gelu(slot_pre.reshape(-1, hidden_width), approximate=False).astype(jnp.bfloat16)
    normed = normalize(slot_conv.reshape(-1, channels))[0].astype(jnp.bfloat16)
    up_sum = lax.dot_general(
        normed, grad_pre, (((0,), (0,)), ((), ())), preferred_element_type=jnp.float32
    )
    down_sum = lax.dot_general(
        hidden, scaled, (((0,), (0,)), ((), ())), preferred_element_type=jnp.float32
    )
    kernel_sum = sum(kernel_grad(slot_in[m], grad_conv[m], kernel) for m in range(micro_count))
    scale_sum = jnp.sum(out_rows * slot_branch.reshape(-1, channels), axis=0)
    parts = [part.reshape(-1, GRAN) for part in (kernel_sum, up_sum, down_sum, scale_sum)]
    row_count = sum(part.shape[0] for part in parts)
    unit_count = -(-row_count // replica_count) * replica_count
    slot_count = master.shape[1]
    step = 128
    slot_rows = -(-slot_count // 16) * 16
    spread = spread_rows(
        parts, bucket_bounds[0], bucket_owner[0], replica_count, unit_count, slot_rows, step
    )
    grad = lax.psum_scatter(
        spread.reshape(-1, GRAN), "dp", scatter_dimension=0, tiled=True
    )
    new_master, new_first, new_second = adam(
        grad, master, first_moment, second_moment, replica_count
    )
    return (slot_out[None], new_master, new_first, new_second)


def solution(mesh):
    placed = (
        P("dp", None, None, None),
        P("dp", None),
        P("dp", None, None, None),
        P("section", None, None, None),
        P("section", None, None),
        P("section", None, None),
        P("section", None),
        P("section", "dp", None),
        P("section", "dp", None),
        P("section", "dp", None),
        P("section", None),
        P("section", None),
    )
    return jax.shard_map(
        body,
        mesh=mesh,
        in_specs=placed,
        out_specs=(
            P("section", "dp", None, None, None),
            P("section", "dp", None),
            P("section", "dp", None),
            P("section", "dp", None),
        ),
        check_vma=False,
    )
```

time: 933 us -> 594 us (0.64)
  waiting for transfers between devices: 484 us -> 193 us
  local copies, waits for them, and re-layouts: 148 us -> 38.4 us
  matrix products: 113 us -> 188 us
  Pallas kernels: 0 us -> 46.2 us
  starting transfers between devices: 65.5 us -> 23.5 us
  loops' own time: 16.6 us -> 0 us
  other arithmetic: 85.3 us -> 69.3 us
  between operations: 14.3 us -> 25.5 us
    ppermute x10 -> x8, waiting for transfers between devices: 288 us -> 51.1 us  [shifted(): return lax.ppermute(block, axis, route)]
    psum x1 -> x0, waiting for transfers between devices: 195 us -> none  [body(): lax.psum(grad_rows[:unit_count].astype(jnp.bfloat16), 'dp')]
    reduce_scatter x0 -> x1, waiting for transfers between devices: none -> 142 us  [body(): lax.psum_scatter(spread.reshape(-1, GRAN), 'dp', scatter_dimension=0, til...]
    unnamed x10 -> x85, local copies, waits for them, and re-layouts: 73.1 us -> 5.69 us
    pallas_call x0 -> x2, Pallas kernels: none -> 46.2 us  [the longest x1 25 us: spread_rows(): pl.pallas_call(functools.partial(spread_kernel, step), out_shape=jax.Shap...]
    ppermute x10 -> x8, starting transfers between devices: 65.5 us -> 23.4 us  [shifted(): return lax.ppermute(block, axis, route)]
    conv_general_dilated x4 -> x9, matrix products: 28.9 us -> 59.5 us  [depthwise(): lax.conv_general_dilated(inputs, kernel[:, :, None, :], (1, 1), ((reach,...]
    concatenate x2 -> x0, other arithmetic: 27.6 us -> none  [the longest x1 16.7 us: body(): jnp.concatenate([kernel_sum.reshape(-1), up_sum.reshape(-1), down_sum.res...]
  transfers between devices with their start and end apart: 11 -> 9, of which waited for: 11 -> 8; matrix products, arithmetic and copies ran while one was open for 0% -> 5% of each run, Pallas kernels for 0% -> 0%
where the time goes in v1:
time: 594 us; the launch traced here: 584 us
  waiting for transfers between devices  193 us (32%)
  matrix products  188 us (32%)
  other arithmetic  69.3 us (12%)
  Pallas kernels  46.2 us (8%)
  local copies, waits for them, and re-layouts  38.4 us (6%)
  between operations  25.5 us (4%)
  starting transfers between devices  23.5 us (4%)
    reduce_scatter x1, waiting for transfers between devices, body(): lax.psum_scatter(spread.reshape(-1, GRAN), 'dp', scatter_dimension=0, til...  142 us
    conv_general_dilated x9, matrix products, depthwise(): lax.conv_general_dilated(inputs, kernel[:, :, None, :], (1, 1), ((reach,...  59.5 us
    ppermute x8, waiting for transfers between devices, shifted(): return lax.ppermute(block, axis, route)  51.1 us
    dot_general x5, matrix products, block_forward(): branch = jnp.dot(hidden, down_matrix, preferred_element_type=jnp.float32)  42.1 us
    dot_general x5, matrix products, block_backward(): lax.dot_general(scaled, down_matrix, (((1,), (1,)), ((), ())), preferred_...  33 us
    pallas_call x1, Pallas kernels, spread_rows(): pl.pallas_call(functools.partial(spread_kernel, step), out_shape=jax.Shap...  25 us
    ppermute x8, starting transfers between devices, shifted(): return lax.ppermute(block, axis, route)  23.4 us
    reshape x2, local copies, waits for them, and re-layouts, body(): part.reshape(-1, GRAN)  21.9 us
  transfers between devices with their start and end apart: 9, of which 8 were waited for; matrix products, arithmetic and copies ran while one was open for 5% of the time, Pallas kernels for 0%

profile of v1, /device:TPU:0, one launch (start us, length us, event | category | flops | bytes accessed | tf_op | source)
XLA Modules:
  0.0 583.6 jit_solution(8353411078477881778)
XLA Ops:
  15.7 7.8 %fusion.551 = (f32[16,16]{1,0:T(8,128)S(1)}, f32[1,16,16,768]{3,0,2,1:T(1,128)S(1)}) fusion(bf16[7,7,1,768]{3,1,0,2:T(8,128)(2,1)S(1)} %bitcast.482, bf16[1,16,16,768]{3,2,1,0:T(8,128)(2,1)S(1)} %constant_dynamic-slice_fusion.5), kind=kOutput, calls=%fused_computation.812 | convolution fusion | flops 15556352 | bytes 1255936 | tf_op jit(solution)/shard_map/conv_general_dilated | solution.py:31
  32.3 9.8 %broadcast_select_fusion.4 = (bf16[256,768]{1,0:T(8,128)(2,1)}, bf16[256,768]{1,0:T(8,128)(2,1)}, f32[256,768]{1,0:T(8,128)}) fusion(pred[]{:T(512)} %get-tuple-element.528, f32[768]{0:T(1024)S(1)} %reduce.198, f32[1,16,16,768]{3,2,0,1:T(8,128)S(1)} %copy.105, bf16[1,3072,768]{2,1,0:T(8,128)(2,1)S(1)} %bitcast.495, f32[256,3072]{1,0:T(8,128)S(1)} %get-tuple-element.586), kind=kOutput, calls=%fused_computation.537 | convolution fusion | flops 1259864064 | bytes 10226689 | tf_op jit(solution)/shard_map/dot_general | solution.py:60
  42.1 5.7 collective-permute-start
  71.1 7.8 %fusion.552 = (f32[16,16]{1,0:T(8,128)S(1)}, f32[1,16,16,768]{3,0,2,1:T(1,128)S(1)}) fusion(bf16[7,7,1,768]{3,1,0,2:T(8,128)(2,1)S(1)} %bitcast.483, bf16[1,16,16,768]{3,2,1,0:T(8,128)(2,1)S(1)} %bitcast.479), kind=kOutput, calls=%fused_computation.813 | convolution fusion | flops 15556352 | bytes 1255936 | tf_op jit(solution)/shard_map/conv_general_dilated | solution.py:31
  84.1 7.9 %fusion.351 = (bf16[256,768]{1,0:T(8,128)(2,1)S(1)}, f32[256,768]{1,0:T(8,128)S(1)}) fusion(bf16[16,16,768]{2,1,0:T(8,128)(2,1)S(1)} %get-tuple-element.542, f32[768]{0:T(1024)S(1)} %reduce.198, bf16[1,3072,768]{2,1,0:T(8,128)(2,1)S(1)} %bitcast.497, f32[256,3072]{1,0:T(8,128)S(1)} %get-tuple-element.588), kind=kOutput, calls=%fused_computation.421 | convolution fusion | flops 1259864064 | bytes 9440256 | tf_op jit(solution)/shard_map/dot_general | solution.py:60
  97.3 6.5 %collective-permute-done.1 = bf16[16,16,768]{2,1,0:T(8,128)(2,1)S(1)} collective-permute-done((bf16[16,16,768]{2,1,0:T(8,128)(2,1)S(1)}, bf16[16,16,768]{2,1,0:T(8,128)(2,1)S(1)}, u32[]{:S(2)}, u32[]{:S(2)}) %collective-permute-start.1) | collective-permute-done | bytes 393248 | tf_op jit(solution)/shard_map/ppermute | solution.py:26
  104.5 8.2 %fusion.553 = (f32[16,16]{1,0:T(8,128)S(1)}, f32[1,16,16,768]{3,0,2,1:T(1,128)S(1)}) fusion(bf16[7,7,1,768]{3,1,0,2:T(8,128)(2,1)S(1)} %bitcast.484, bf16[1,16,16,768]{3,2,1,0:T(8,128)(2,1)S(1)} %bitcast.477), kind=kOutput, calls=%fused_computation.814 | convolution fusion | flops 15556352 | bytes 1255936 | tf_op jit(solution)/shard_map/conv_general_dilated | solution.py:31
  117.7 7.9 %fusion.350 = (bf16[256,768]{1,0:T(8,128)(2,1)S(1)}, f32[256,768]{1,0:T(8,128)S(1)}) fusion(bf16[16,16,768]{2,1,0:T(8,128)(2,1)S(1)} %get-tuple-element.540, f32[768]{0:T(1024)S(1)} %reduce.198, bf16[1,3072,768]{2,1,0:T(8,128)(2,1)S(1)} %bitcast.497, f32[256,3072]{1,0:T(8,128)S(1)} %get-tuple-element.590), kind=kOutput, calls=%fused_computation.419 | convolution fusion | flops 1259864064 | bytes 9440256 | tf_op jit(solution)/shard_map/dot_general | solution.py:60
  131.7 5.5 collective-permute-done.2
  138.0 8.0 %fusion.554 = (f32[16,16]{1,0:T(8,128)S(1)}, f32[1,16,16,768]{3,0,2,1:T(1,128)S(1)}) fusion(bf16[7,7,1,768]{3,1,0,2:T(8,128)(2,1)S(1)} %bitcast.485, bf16[1,16,16,768]{3,2,1,0:T(8,128)(2,1)S(1)} %bitcast.478), kind=kOutput, calls=%fused_computation.815 | convolution fusion | flops 15556352 | bytes 1255936 | tf_op jit(solution)/shard_map/conv_general_dilated | solution.py:31
  150.9 7.9 %fusion.349 = (bf16[256,768]{1,0:T(8,128)(2,1)S(1)}, f32[256,768]{1,0:T(8,128)S(1)}) fusion(bf16[16,16,768]{2,1,0:T(8,128)(2,1)S(1)} %get-tuple-element.538, f32[768]{0:T(1024)S(1)} %reduce.198, bf16[1,3072,768]{2,1,0:T(8,128)(2,1)S(1)} %bitcast.497, f32[256,3072]{1,0:T(8,128)S(1)} %get-tuple-element.592), kind=kOutput, calls=%fused_computation.417 | convolution fusion | flops 1259864064 | bytes 9440256 | tf_op jit(solution)/shard_map/dot_general | solution.py:60
  170.2 8.0 %fusion.555 = (f32[16,16]{1,0:T(8,128)S(1)}, f32[1,16,16,768]{3,0,2,1:T(1,128)S(1)}) fusion(bf16[7,7,1,768]{3,1,0,2:T(8,128)(2,1)S(1)} %bitcast.486, bf16[1,16,16,768]{3,2,1,0:T(8,128)(2,1)S(1)} %bitcast.476), kind=kOutput, calls=%fused_computation.816 | convolution fusion | flops 15556352 | bytes 1255936 | tf_op jit(solution)/shard_map/conv_general_dilated | solution.py:31
  183.3 8.6 %fusion.348 = (bf16[256,768]{1,0:T(8,128)(2,1)}, f32[256,768]{1,0:T(8,128)S(1)}) fusion(bf16[16,16,768]{2,1,0:T(8,128)(2,1)S(1)} %get-tuple-element.536, f32[768]{0:T(1024)S(1)} %reduce.198, bf16[1,3072,768]{2,1,0:T(8,128)(2,1)S(1)} %bitcast.497, f32[256,3072]{1,0:T(8,128)S(1)} %get-tuple-element.594), kind=kOutput, calls=%fused_computation.415 | convolution fusion | flops 1259864064 | bytes 9440256 | tf_op jit(solution)/shard_map/dot_general | solution.py:60
  193.8 14.7 %fusion.2 = (bf16[2,256,3072]{2,1,0:T(8,128)(2,1)}, f32[2,256,3072]{2,1,0:T(8,128)S(1)}) fusion(f32[3,256,3072]{2,1,0:T(8,128)S(1)} %get-tuple-element.593), kind=kLoop, calls=%fused_computation.3 | loop fusion | flops 102236160 | bytes 15728640 | tf_op jit(solution)/shard_map/convert_element_type | solution.py:302
  218.8 5.2 fusion.334
  227.0 8.5 %collective-permute-done.4 = bf16[16,16,768]{2,1,0:T(8,128)(2,1)S(1)} collective-permute-done((bf16[16,16,768]{2,1,0:T(8,128)(2,1)S(1)}, bf16[16,16,768]{2,1,0:T(8,128)(2,1)S(1)}, u32[]{:S(2)}, u32[]{:S(2)}) %collective-permute-start.4) | collective-permute-done | bytes 393248 | tf_op jit(solution)/shard_map/ppermute | solution.py:26
  236.3 7.7 %fusion.179 = (bf16[3,256,3072]{2,1,0:T(8,128)(2,1)S(1)}, bf16[256,3072]{1,0:T(8,128)(2,1)}) fusion(bf16[3,256,3072]{2,1,0:T(8,128)(2,1)S(1)} %get-tuple-element.600, s32[]{:T(128)} %select_n.213, pred[]{:T(512)} %get-tuple-element.557, f32[2,256,3072]{2,1,0:T(8,128)S(1)} %get-tuple-element.546, s32[]{:T(128)S(6)} %min.37, ...), kind=kOutput, calls=%fused_computation.229 | convolution fusion | flops 1216610304 | bytes 12976137 | tf_op jit(solution)/shard_map/dot_general | solution.py:71
  253.6 9.7 %collective-permute-done.5 = bf16[16,16,768]{2,1,0:T(8,128)(2,1)S(1)} collective-permute-done((bf16[16,16,768]{2,1,0:T(8,128)(2,1)S(1)}, bf16[16,16,768]{2,1,0:T(8,128)(2,1)S(1)}, u32[]{:S(2)}, u32[]{:S(2)}) %collective-permute-start.5) | collective-permute-done | bytes 393248 | tf_op jit(solution)/shard_map/ppermute | solution.py:26
  264.3 7.5 %fusion.178 = (bf16[3,256,3072]{2,1,0:T(8,128)(2,1)S(1)}, bf16[256,3072]{1,0:T(8,128)(2,1)}) fusion(bf16[3,256,3072]{2,1,0:T(8,128)(2,1)S(1)} %get-tuple-element.602, s32[]{:T(128)} %select_n.218, pred[]{:T(512)} %get-tuple-element.558, f32[2,256,3072]{2,1,0:T(8,128)S(1)} %get-tuple-element.546, s32[]{:T(128)S(6)} %min.38, ...), kind=kOutput, calls=%fused_computation.227 | convolution fusion | flops 1216610304 | bytes 12976137 | tf_op jit(solution)/shard_map/dot_general | solution.py:71
  282.1 8.6 %collective-permute-done.6 = bf16[16,16,768]{2,1,0:T(8,128)(2,1)S(1)} collective-permute-done((bf16[16,16,768]{2,1,0:T(8,128)(2,1)S(1)}, bf16[16,16,768]{2,1,0:T(8,128)(2,1)S(1)}, u32[]{:S(2)}, u32[]{:S(2)}) %collective-permute-start.6) | collective-permute-done | bytes 393248 | tf_op jit(solution)/shard_map/ppermute | solution.py:26
  291.6 7.8 %fusion.177 = (bf16[3,256,3072]{2,1,0:T(8,128)(2,1)S(1)}, bf16[256,3072]{1,0:T(8,128)(2,1)}) fusion(bf16[3,256,3072]{2,1,0:T(8,128)(2,1)S(1)} %get-tuple-element.604, s32[]{:T(128)} %select_n.222, pred[]{:T(512)} %get-tuple-element.510, f32[2,256,3072]{2,1,0:T(8,128)S(1)} %get-tuple-element.546, s32[]{:T(128)S(6)} %min.39, ...), kind=kOutput, calls=%fused_computation.225 | convolution fusion | flops 1216610304 | bytes 12976137 | tf_op jit(solution)/shard_map/dot_general | solution.py:71
  310.5 7.7 %collective-permute-done.7 = bf16[16,16,768]{2,1,0:T(8,128)(2,1)S(1)} collective-permute-done((bf16[16,16,768]{2,1,0:T(8,128)(2,1)S(1)}, bf16[16,16,768]{2,1,0:T(8,128)(2,1)S(1)}, u32[]{:S(2)}, u32[]{:S(2)}) %collective-permute-start.7) | collective-permute-done | bytes 393248 | tf_op jit(solution)/shard_map/ppermute | solution.py:26
  321.4 5.1 fusion.176
  329.8 7.6 %fusion.330 = f32[1,7,7,768]{3,0,2,1:T(1,128)S(1)} fusion(bf16[1,22,22,768]{3,2,1,0:T(8,128)(2,1)S(1)} %get-tuple-element.612, bf16[16,16,1,768]{3,1,0,2:T(8,128)(2,1)S(1)} %get-tuple-element.550), kind=kOutput, calls=%fused_computation.388 | convolution fusion | flops 19267584 | bytes 1287168 | tf_op jit(solution)/shard_map/conv_general_dilated | solution.py:95
  337.4 7.6 %fusion.338 = f32[7,7,768]{2,1,0:T(8,128)S(1)} fusion(f32[1,7,7,768]{3,0,2,1:T(1,128)S(1)} %fusion.330, bf16[1,22,22,768]{3,2,1,0:T(8,128)(2,1)S(1)} %get-tuple-element.613, bf16[16,16,1,768]{3,1,0,2:T(8,128)(2,1)S(1)} %get-tuple-element.549), kind=kOutput, calls=%fused_computation.395 | convolution fusion | flops 19305216 | bytes 1437696 | tf_op jit(solution)/shard_map/conv_general_dilated | solution.py:95
  345.7 7.2 %convolution_bitcast_fusion = f32[768,3072]{1,0:T(8,128)} fusion(bf16[3,256,3072]{2,1,0:T(8,128)(2,1)} %copy-done.3, f32[2,256]{1,0:T(2,128)S(1)} %add_rsqrt_fusion.5, f32[2,256]{1,0:T(2,128)S(1)} %broadcast_multiply_fusion.5, f32[3,256,768]{2,1,0:T(8,128)S(1)} %select_dynamic-update-slice_fusion), kind=kOutput, calls=%fused_computation.19 | convolution fusion | flops 2417098752 | bytes 14159872 | tf_op jit(solution)/shard_map/dot_general | solution.py:304
  352.9 11.1 %reshape.1809.refs_1_ = f32[18432,128]{1,0:T(8,128)} reshape(f32[768,3072]{1,0:T(8,128)} %convolution_bitcast_fusion) | data formatting | bytes 18874368 | tf_op jit(solution)/shard_map/reshape | solution.py:312
  364.0 6.2 %fusion.556 = f32[3072,768]{1,0:T(8,128)} fusion(bf16[512,3072]{1,0:T(8,128)(2,1)S(1)} %bitcast.447, bf16[512,768]{1,0:T(8,128)(2,1)} %bitcast.462), kind=kOutput, calls=%fused_computation.817 | convolution fusion | flops 2415919104 | bytes 13369344 | tf_op jit(solution)/shard_map/dot_general | solution.py:307
  370.2 10.9 %reshape.1814.refs_2_ = f32[18432,128]{1,0:T(8,128)} reshape(f32[3072,768]{1,0:T(8,128)} %fusion.556) | data formatting | bytes 18874368 | tf_op jit(solution)/shard_map/reshape | solution.py:312
  383.2 25.0 %spread_rows.1 = bf16[8,6976,128]{2,1,0:T(8,128)(2,1)} custom-call(s32[25]{0:T(128)} %bitcast.492, s32[24]{0:T(128)} %bitcast.493, f32[294,128]{1,0:T(8,128)} %add.386.refs_0_, f32[18432,128]{1,0:T(8,128)} %reshape.1809.refs_1_, f32[18432,128]{1,0:T(8,128)} %reshape.1814.refs_2_, f32[6,128]{1,0:T(8,128)} %bitcast.491), custom_call_target="tpu_custom_call" | custom-call | tf_op jit(solution)/shard_map/spread_rows/pallas_call | solution.py:154
  413.4 141.9 %reduce-scatter.2.cloned.1.call-done.grad_ref = bf16[6976,128]{1,0:T(8,128)(2,1)} async-done(((bf16[55808,128]{1,0:T(8,128)(2,1)}), bf16[6976,128]{1,0:T(8,128)(2,1)}) %reduce-scatter.2.cloned.1.call-update) | async-done | bytes 1785872 | tf_op jit(solution)/shard_map/reduce_scatter | solution.py:321
  555.3 21.2 %adam.1 = (f32[6969,1,128]{2,1,0:T(1,128)}, f32[6969,1,128]{2,1,0:T(1,128)}, f32[6969,1,128]{2,1,0:T(1,128)}) custom-call(bf16[6976,128]{1,0:T(8,128)(2,1)} %reduce-scatter.2.cloned.1.call-done.grad_ref, f32[6969,1,128]{2,1,0:T(1,128)} %bitcast.440, f32[6969,1,128]{2,1,0:T(1,128)} %bitcast.441, f32[6969,1,128]{2,1,0:T(1,128)} %bitcast.442), custom_call_target="tpu_custom_call" | custom-call | tf_op jit(solution)/shard_map/adam/pallas_call | solution.py:196
  (233 shorter events, 137.4 us)
Async XLA Ops:
  7.2 7.8 %copy-start.24 = (s32[3]{0:T(128)S(1)}, s32[3]{0:T(128)}, u32[]{:S(2)}) copy-start(s32[3]{0:T(128)} %constant.985.clone.1) | copy-start | bytes 40
  7.2 8.5 %copy-start.20 = (bf16[1,7,7,768]{3,2,1,0:T(8,128)(2,1)S(1)}, bf16[1,7,7,768]{3,2,1,0:T(8,128)(2,1)}, u32[]{:S(2)}) copy-start(bf16[1,7,7,768]{3,2,1,0:T(8,128)(2,1)} %param.95) | copy-start | bytes 225796
  7.2 548.1 %reduce-scatter.2.cloned.1.call-start = ((), (), s32[]{:S(2)}) async-start(), calls=%async_computation.1 | async-start | bytes 16072704 | tf_op jit(solution)/shard_map/reduce_scatter | solution.py:321
  23.5 4.2 copy-start.25
  27.7 4.6 slice-start.7
  32.3 9.8 %copy-start = (f32[3,256,3072]{2,1,0:T(8,128)}, f32[3,256,3072]{2,1,0:T(8,128)S(1)}, u32[]{:S(2)}) copy-start(f32[3,256,3072]{2,1,0:T(8,128)S(1)} %get-tuple-element.585) | copy-start | bytes 28311556
  32.3 15.6 %copy-start.23 = (s32[4]{0:T(128)S(1)}, s32[4]{0:T(128)}, u32[]{:S(2)}) copy-start(s32[4]{0:T(128)} %constant.950.clone.1) | copy-start | bytes 52
  32.3 17.9 %copy-start.4 = (bf16[2,16,16,768]{3,2,1,0:T(8,128)(2,1)S(1)}, bf16[2,16,16,768]{3,2,1,0:T(8,128)(2,1)}, u32[]{:S(2)}) copy-start(bf16[2,16,16,768]{3,2,1,0:T(8,128)(2,1)} %param.94) | copy-start | bytes 2359300
  42.1 28.0 %collective-permute-start = (bf16[16,16,768]{2,1,0:T(8,128)(2,1)}, bf16[16,16,768]{2,1,0:T(8,128)(2,1)}, u32[]{:S(2)}, u32[]{:S(2)}) collective-permute-start(bf16[16,16,768]{2,1,0:T(8,128)(2,1)} %bitcast.9), channel_id=1, source_target_pairs={{0,8},{8,16},{16,24},{1,9},{9,17},{17,25},{2,10},{10,18},{18,26},{... | collective-permute-start | bytes 1179656 | tf_op jit(solution)/shard_map/ppermute | solution.py:26
  67.3 2.9 copy-start.6
  67.3 3.8 copy-start.21
  71.0 10.4 %slice-start.2 = ((s8[4718592]{0:T(1024)(128)(4,1)}), s8[4194304]{0:T(1024)(128)(4,1)S(1)}, s32[]{:S(2)}) async-start(s8[4718592]{0:T(1024)(128)(4,1)} %bitcast.434), calls=%async_computation.4 | async-start | bytes 8388608
  71.0 10.4 %slice-start.4 = ((s8[9437184]{0:T(1024)(128)(4,1)}), s8[4194304]{0:T(1024)(128)(4,1)S(1)}, s32[]{:S(2)}) async-start(s8[9437184]{0:T(1024)(128)(4,1)} %bitcast.436), calls=%async_computation.6 | async-start | bytes 8388608
  71.0 10.4 %slice-start.3 = ((s8[4718592]{0:T(1024)(128)(4,1)}), s8[524288]{0:T(1024)(128)(4,1)S(1)}, s32[]{:S(2)}) async-start(s8[4718592]{0:T(1024)(128)(4,1)} %bitcast.434), calls=%async_computation.5 | async-start | bytes 1048576
  71.0 10.4 %slice-start.5 = ((s8[9437184]{0:T(1024)(128)(4,1)}), s8[4194304]{0:T(1024)(128)(4,1)S(1)}, s32[]{:S(2)}) async-start(s8[9437184]{0:T(1024)(128)(4,1)} %bitcast.436), calls=%async_computation.7 | async-start | bytes 8388608
  71.0 10.4 %slice-start.6 = ((s8[9437184]{0:T(1024)(128)(4,1)}), s8[1048576]{0:T(1024)(128)(4,1)S(1)}, s32[]{:S(2)}) async-start(s8[9437184]{0:T(1024)(128)(4,1)} %bitcast.436), calls=%async_computation.8 | async-start | bytes 2097152
  80.4 3.6 slice-start.9
  92.0 12.6 %copy-start.12 = (bf16[256,768]{1,0:T(8,128)(2,1)}, bf16[256,768]{1,0:T(8,128)(2,1)S(1)}, u32[]{:S(2)}) copy-start(bf16[256,768]{1,0:T(8,128)(2,1)S(1)} %get-tuple-element.571) | copy-start | bytes 1179652
  92.0 11.7 %collective-permute-start.1 = (bf16[16,16,768]{2,1,0:T(8,128)(2,1)S(1)}, bf16[16,16,768]{2,1,0:T(8,128)(2,1)S(1)}, u32[]{:S(2)}, u32[]{:S(2)}) collective-permute-start(bf16[16,16,768]{2,1,0:T(8,128)(2,1)S(1)} %bitcast.467), channel_id=1, source_target_pairs={{0,8},{8,16},{16,24},{1,9},{9,17},{17,25},{2,10},{10,18},{18,26},{... | collective-permute-start | bytes 1179656 | tf_op jit(solution)/shard_map/ppermute | solution.py:26
  125.6 12.4 %copy-start.14 = (bf16[256,768]{1,0:T(8,128)(2,1)}, bf16[256,768]{1,0:T(8,128)(2,1)S(1)}, u32[]{:S(2)}) copy-start(bf16[256,768]{1,0:T(8,128)(2,1)S(1)} %get-tuple-element.575) | copy-start | bytes 1179652
  125.6 11.6 %collective-permute-start.2 = (bf16[16,16,768]{2,1,0:T(8,128)(2,1)S(1)}, bf16[16,16,768]{2,1,0:T(8,128)(2,1)S(1)}, u32[]{:S(2)}, u32[]{:S(2)}) collective-permute-start(bf16[16,16,768]{2,1,0:T(8,128)(2,1)S(1)} %bitcast.469), channel_id=1, source_target_pairs={{0,8},{8,16},{16,24},{1,9},{9,17},{17,25},{2,10},{10,18},{18,26},{... | collective-permute-start | bytes 1179656 | tf_op jit(solution)/shard_map/ppermute | solution.py:26
  158.8 11.5 %copy-start.16 = (bf16[256,768]{1,0:T(8,128)(2,1)}, bf16[256,768]{1,0:T(8,128)(2,1)S(1)}, u32[]{:S(2)}) copy-start(bf16[256,768]{1,0:T(8,128)(2,1)S(1)} %get-tuple-element.579) | copy-start | bytes 1179652
  158.8 10.6 %collective-permute-start.3 = (bf16[16,16,768]{2,1,0:T(8,128)(2,1)S(1)}, bf16[16,16,768]{2,1,0:T(8,128)(2,1)S(1)}, u32[]{:S(2)}, u32[]{:S(2)}) collective-permute-start(bf16[16,16,768]{2,1,0:T(8,128)(2,1)S(1)} %bitcast.471), channel_id=1, source_target_pairs={{0,8},{8,16},{16,24},{1,9},{9,17},{17,25},{2,10},{10,18},{18,26},{... | collective-permute-start | bytes 1179656 | tf_op jit(solution)/shard_map/ppermute | solution.py:26
  224.1 11.4 %collective-permute-start.4 = (bf16[16,16,768]{2,1,0:T(8,128)(2,1)S(1)}, bf16[16,16,768]{2,1,0:T(8,128)(2,1)S(1)}, u32[]{:S(2)}, u32[]{:S(2)}) collective-permute-start(bf16[16,16,768]{2,1,0:T(8,128)(2,1)S(1)} %bitcast.475), channel_id=1, source_target_pairs={{8,0},{16,8},{24,16},{9,1},{17,9},{25,17},{10,2},{18,10},{26,18},{... | collective-permute-start | bytes 1179656 | tf_op jit(solution)/shard_map/ppermute | solution.py:26
  225.7 9.8 %copy-start.5 = (bf16[2,16,16,768]{3,2,1,0:T(8,128)(2,1)S(1)}, bf16[2,16,16,768]{3,2,1,0:T(8,128)(2,1)}, u32[]{:S(2)}) copy-start(bf16[2,16,16,768]{3,2,1,0:T(8,128)(2,1)} %param.94) | copy-start | bytes 2359300
  227.0 17.0 %copy-start.1 = (f32[3,256,768]{2,1,0:T(8,128)}, f32[3,256,768]{2,1,0:T(8,128)S(1)}, u32[]{:S(2)}) copy-start(f32[3,256,768]{2,1,0:T(8,128)S(1)} %fusion.352) | copy-start | bytes 7077892
  252.3 11.0 %collective-permute-start.5 = (bf16[16,16,768]{2,1,0:T(8,128)(2,1)S(1)}, bf16[16,16,768]{2,1,0:T(8,128)(2,1)S(1)}, u32[]{:S(2)}, u32[]{:S(2)}) collective-permute-start(bf16[16,16,768]{2,1,0:T(8,128)(2,1)S(1)} %fusion.342), channel_id=1, source_target_pairs={{8,0},{16,8},{24,16},{9,1},{17,9},{25,17},{10,2},{18,10},{26,18},{... | collective-permute-start | bytes 1179656 | tf_op jit(solution)/shard_map/ppermute | solution.py:26
  280.1 10.6 %collective-permute-start.6 = (bf16[16,16,768]{2,1,0:T(8,128)(2,1)S(1)}, bf16[16,16,768]{2,1,0:T(8,128)(2,1)S(1)}, u32[]{:S(2)}, u32[]{:S(2)}) collective-permute-start(bf16[16,16,768]{2,1,0:T(8,128)(2,1)S(1)} %fusion.344), channel_id=1, source_target_pairs={{8,0},{16,8},{24,16},{9,1},{17,9},{25,17},{10,2},{18,10},{26,18},{... | collective-permute-start | bytes 1179656 | tf_op jit(solution)/shard_map/ppermute | solution.py:26
  307.6 10.6 %collective-permute-start.7 = (bf16[16,16,768]{2,1,0:T(8,128)(2,1)S(1)}, bf16[16,16,768]{2,1,0:T(8,128)(2,1)S(1)}, u32[]{:S(2)}, u32[]{:S(2)}) collective-permute-start(bf16[16,16,768]{2,1,0:T(8,128)(2,1)S(1)} %fusion.346), channel_id=1, source_target_pairs={{8,0},{16,8},{24,16},{9,1},{17,9},{25,17},{10,2},{18,10},{26,18},{... | collective-permute-start | bytes 1179656 | tf_op jit(solution)/shard_map/ppermute | solution.py:26
  352.9 11.1 %copy-start.10 = (bf16[2,256,3072]{2,1,0:T(8,128)(2,1)S(1)}, bf16[2,256,3072]{2,1,0:T(8,128)(2,1)}, u32[]{:S(2)}) copy-start(bf16[2,256,3072]{2,1,0:T(8,128)(2,1)} %get-tuple-element.545) | copy-start | bytes 9437188
  370.2 10.9 %copy-start.2 = (f32[3,256,768]{2,1,0:T(8,128)S(1)}, f32[3,256,768]{2,1,0:T(8,128)}, u32[]{:S(2)}) copy-start(f32[3,256,768]{2,1,0:T(8,128)} %copy-done.1) | copy-start | bytes 7077892
  408.3 3.4 copy-start.18
  (14 other events, 27.1 us)
Sparse Core Ops, SparseCore 0:
  408.4 146.8 reduce-scatter.1
